TPU v7x, 32 devices: a whole 2x2x4 slice. The times are simulated.
32 devices in a mesh: groups: 2 (over y), space: 4 (over z), src: 4 (over x, core).
Axes of the slice: x: 2, y: 2, z: 4, core: 2. Of those that a mesh axis runs over, the one named last changes fastest.
Arguments:
- conductivity: float32 [32, 64, 256], P(('groups', 'space')), parts along dimension 0, may hold values from 0.2 to 5
- inverse_coefficients: float32 [27, 32, 64, 256], P(None, ('groups', 'space')), parts along dimension 1
- forward_potential: float32 [16, 16, 64, 256], P(('groups', 'src'), 'space'), parts along dimension 0, may hold values from -6 to 6
- misfit_field: float32 [16, 16, 64, 256], P(('groups', 'src'), 'space'), parts along dimension 0
- electrodes: int32 [16, 2], P(('groups', 'src')), parts along dimension 0, may hold values from 0 to 262143
- assignment: int32 [16], P(('groups', 'src')), parts along dimension 0, may hold values from 0 to 3
- line_weight: float32 [8], P('groups'), parts along dimension 0, may hold values from 0.5 to 2
Outputs:
- adjoint_field: float32 [16, 16, 64, 256], P(('groups', 'src'), 'space'), parts along dimension 0
- gradient: float32 [32, 64, 256], P(('groups', 'space'), 'src'), parts along dimension 0
There are 2 independent parts, one for each index of `groups`. A program takes and returns all parts, laid end to end along the dimension named above; each array names one. Nothing has to cross between parts.
All inputs are finite; a program needn't handle non-finite values.
Results may differ from a plain program's by a relative error of at most 0.0001.
Values sent between devices are 32-bit elements; how exact they have to be, the bound alone decides.
A program may use at most 128 MiB of HBM per device.

v0:
```python
import jax
import jax.numpy as jnp
from jax import lax
from jax.sharding import PartitionSpec as P

ITERS = 2


mass_shift = 0.05
current = 5.0
stencil_offsets = tuple(
    (
        (step_x - 1, step_y - 1, step_z - 1)
        for step_x in range(3)
        for step_y in range(3)
        for step_z in range(3)
    )
)
face_offsets = ((1, 0, 0), (-1, 0, 0), (0, 1, 0), (0, -1, 0), (0, 0, 1), (0, 0, -1))


def extended(cells, sides, width):
    for axis, dim in sides:
        count = lax.axis_size(axis)
        ends = count - 1
        head = lax.slice_in_dim(cells, 0, width, axis=dim)
        tail = lax.slice_in_dim(cells, cells.shape[dim] - width, cells.shape[dim], axis=dim)
        cells = jnp.concatenate(
            [
                lax.ppermute(tail, axis, [(i, (i + 1) % count) for i in range(ends)]),
                cells,
                lax.ppermute(head, axis, [((i + 1) % count, i) for i in range(ends)]),
            ],
            axis=dim,
        )
    return cells


def pad_sides(field_in):
    return jnp.pad(field_in, ((0, 0), (0, 0), (1, 1), (1, 1)))


def operate_padded(padded, sigma_pad, slab_rows, height, depth_cells):
    center = padded[:, 1 : 1 + slab_rows, 1 : 1 + height, 1 : 1 + depth_cells]
    sigma_center = sigma_pad[1 : 1 + slab_rows, 1 : 1 + height, 1 : 1 + depth_cells]
    accumulated = mass_shift * center
    for step_x, step_y, step_z in face_offsets:
        beside = padded[
            :,
            1 + step_x : 1 + step_x + slab_rows,
            1 + step_y : 1 + step_y + height,
            1 + step_z : 1 + step_z + depth_cells,
        ]
        sigma_beside = sigma_pad[
            1 + step_x : 1 + step_x + slab_rows,
            1 + step_y : 1 + step_y + height,
            1 + step_z : 1 + step_z + depth_cells,
        ]
        accumulated = accumulated + 0.5 * (sigma_center + sigma_beside) * (center - beside)
    return accumulated


def apply_forward(padded, coef_slab, slab_rows, height, depth_cells):
    accumulated = jnp.zeros((padded.shape[0], slab_rows, height, depth_cells), jnp.float32)
    for position, (step_x, step_y, step_z) in enumerate(stencil_offsets):
        accumulated = (
            accumulated
            + coef_slab[position]
            * padded[
                :,
                1 + step_x : 1 + step_x + slab_rows,
                1 + step_y : 1 + step_y + height,
                1 + step_z : 1 + step_z + depth_cells,
            ]
        )
    return accumulated


def apply_transposed(padded, coef_pad, slab_rows, height, depth_cells):
    accumulated = jnp.zeros((padded.shape[0], slab_rows, height, depth_cells), jnp.float32)
    for position, (step_x, step_y, step_z) in enumerate(stencil_offsets):
        coef_part = coef_pad[
            position,
            1 - step_x : 1 - step_x + slab_rows,
            1 - step_y : 1 - step_y + height,
            1 - step_z : 1 - step_z + depth_cells,
        ]
        field_part = padded[
            :,
            1 - step_x : 1 - step_x + slab_rows,
            1 - step_y : 1 - step_y + height,
            1 - step_z : 1 - step_z + depth_cells,
        ]
        accumulated = accumulated + coef_part * field_part
    return accumulated


def face_products(forward_pad, adjoint_pad, slab_rows, height, depth_cells):
    fwd_center = forward_pad[:, 1 : 1 + slab_rows, 1 : 1 + height, 1 : 1 + depth_cells]
    adj_center = adjoint_pad[:, 1 : 1 + slab_rows, 1 : 1 + height, 1 : 1 + depth_cells]
    accumulated = jnp.zeros(fwd_center.shape, jnp.float32)
    for step_x, step_y, step_z in face_offsets:
        fwd_beside = forward_pad[
            :,
            1 + step_x : 1 + step_x + slab_rows,
            1 + step_y : 1 + step_y + height,
            1 + step_z : 1 + step_z + depth_cells,
        ]
        adj_beside = adjoint_pad[
            :,
            1 + step_x : 1 + step_x + slab_rows,
            1 + step_y : 1 + step_y + height,
            1 + step_z : 1 + step_z + depth_cells,
        ]
        accumulated = accumulated + (fwd_center - fwd_beside) * (adj_center - adj_beside)
    return accumulated


def local_sums(first_field, second_field):
    return jnp.sum(first_field * second_field, axis=(1, 2, 3))


def aligned_total(residual, smoothed):
    return lax.psum(local_sums(residual, smoothed), "space")


def body(
    conductivity,
    inverse_coefficients,
    forward_potential,
    misfit_field,
    electrodes,
    assignment,
    line_weight,
):
    sources, slab_rows, height, depth_cells = misfit_field.shape
    local_cells = slab_rows * height * depth_cells
    offset = lax.axis_index("space") * local_cells
    shifted = electrodes - offset
    inside_slab = (shifted >= 0) & (shifted < local_cells)
    target = jnp.where(inside_slab, shifted, local_cells)
    source_rows = jnp.arange(sources, dtype=jnp.int32)
    charges = jnp.array([current, -current], jnp.float32)
    flattened = (
        misfit_field.reshape(sources, local_cells)
        .at[source_rows[:, None], target]
        .add(charges[None, :], mode="drop")
    )
    right_side = flattened.reshape(misfit_field.shape)
    sigma_ext, coef_ext = (
        extended(conductivity[None], (("space", 1),), 1),
        extended(inverse_coefficients, (("space", 1),), 1),
    )
    sigma_pad = pad_sides(sigma_ext)[0]
    coef_pad = pad_sides(coef_ext)

    def operate(field_in):
        padded = pad_sides(extended(field_in, (("space", 1),), 1))
        return operate_padded(padded, sigma_pad, slab_rows, height, depth_cells)

    def precondition(field_in):
        padded = pad_sides(extended(field_in, (("space", 1),), 1))
        smooth = apply_forward(padded, inverse_coefficients, slab_rows, height, depth_cells)
        smooth_pad = pad_sides(extended(smooth, (("space", 1),), 1))
        return apply_transposed(smooth_pad, coef_pad, slab_rows, height, depth_cells)

    adjoint = jnp.zeros_like(right_side)
    residual = right_side
    smoothed = precondition(residual)
    align_now = aligned_total(residual, smoothed)
    direction = smoothed
    for iteration in range(ITERS):
        image_field = operate(direction)
        step_size = align_now / lax.psum(local_sums(direction, image_field), "space")
        adjoint = adjoint + step_size[:, None, None, None] * direction
        residual = residual - step_size[:, None, None, None] * image_field
        if iteration + 1 < ITERS:
            smoothed = precondition(residual)
            align_next = aligned_total(residual, smoothed)
            growth = align_next / align_now
            direction = smoothed + growth[:, None, None, None] * direction
            align_now = align_next
    lines = jnp.arange(line_weight.shape[0], dtype=jnp.int32)
    weights = jnp.sum(
        line_weight[None, :] * (assignment[:, None] == lines[None, :]).astype(jnp.float32), axis=1
    )
    fwd_ext, adj_ext = (
        extended(forward_potential, (("space", 1),), 1),
        extended(adjoint, (("space", 1),), 1),
    )
    products = face_products(pad_sides(fwd_ext), pad_sides(adj_ext), slab_rows, height, depth_cells)
    local_term = -0.5 * jnp.sum(weights[:, None, None, None] * products, axis=0)
    gradient = lax.psum_scatter(local_term, "src", scatter_dimension=1, tiled=True)
    return (adjoint, gradient)


def solution(mesh):
    in_specs = (
        P(("groups", "space"), None, None),
        P(None, ("groups", "space"), None, None),
        P(("groups", "src"), "space", None, None),
        P(("groups", "src"), "space", None, None),
        P(("groups", "src"), None),
        P(("groups", "src")),
        P("groups"),
    )
    out_specs = (P(("groups", "src"), "space", None, None), P(("groups", "space"), "src", None))
    return jax.shard_map(body, mesh=mesh, in_specs=in_specs, out_specs=out_specs, check_vma=False)
```

profile of v0, /device:TPU:1, one launch (start us, length us, event | category | flops | bytes accessed | tf_op | source)
XLA Modules:
  0.0 222.5 jit_solution(5572397916608157558)
XLA Ops:
  7.2 4.5 %fusion.183 = (f32[27,1,64,256]{3,2,1,0:T(8,128)}, f32[27,1,64,256]{3,2,1,0:T(8,128)}) fusion(f32[27,4,64,256]{3,2,1,0:T(8,128)} %param.9), kind=kLoop, calls=%fused_computation.414 | loop fusion | bytes 7077888 | tf_op jit(solution)/shard_map/slice | solution.py:27
  13.1 5.9 %collective-permute-start = (f32[27,1,64,256]{3,2,1,0:T(8,128)}, f32[27,1,64,256]{3,2,1,0:T(8,128)}, u32[]{:S(2)}, u32[]{:S(2)}) collective-permute-start(f32[27,1,64,256]{3,2,1,0:T(8,128)} %get-tuple-element.62), channel_id=1, source_target_pairs={{0,4},{4,8},{8,12},{1,5},{5,9},{9,13},{2,6},{6,10},{10,14},{3,7},{... | collective-permute-start | bytes 5308424 | tf_op jit(solution)/shard_map/ppermute | solution.py:30
  19.6 2.1 collective-permute-start.6
  24.5 4.0 %collective-permute-start.2 = (f32[2,1,64,256]{3,2,1,0:T(8,128)S(1)}, f32[2,1,64,256]{3,2,1,0:T(8,128)S(1)}, u32[]{:S(2)}, u32[]{:S(2)}) collective-permute-start(f32[2,1,64,256]{3,2,1,0:T(8,128)S(1)} %get-tuple-element.84), channel_id=1, source_target_pairs={{0,4},{4,8},{8,12},{1,5},{5,9},{9,13},{2,6},{6,10},{10,14},{3,7},{... | collective-permute-start | bytes 393224 | tf_op jit(solution)/shard_map/ppermute | solution.py:30
  28.5 28.3 %collective-permute-done.6 = f32[1,1,64,256]{3,2,1,0:T(8,128)S(1)} collective-permute-done((f32[1,1,64,256]{3,2,1,0:T(8,128)}, f32[1,1,64,256]{3,2,1,0:T(8,128)S(1)}, u32[]{:S(2)}, u32[]{:S(2)}) %collective-permute-start.6) | collective-permute-done | bytes 65568 | tf_op jit(solution)/shard_map/ppermute | solution.py:30
  59.5 3.7 %collective-permute-done.3 = f32[2,1,64,256]{3,2,1,0:T(8,128)S(1)} collective-permute-done((f32[2,1,64,256]{3,2,1,0:T(8,128)S(1)}, f32[2,1,64,256]{3,2,1,0:T(8,128)S(1)}, u32[]{:S(2)}, u32[]{:S(2)}) %collective-permute-start.3) | collective-permute-done | bytes 131104 | tf_op jit(solution)/shard_map/ppermute | solution.py:32
  63.7 4.4 %fusion.176 = (f32[4,64,256]{2,1,0:T(8,128)}, f32[4,64,256]{2,1,0:T(8,128)S(1)}, f32[4,64,256]{2,1,0:T(8,128)S(1)}, f32[4,64,256]{2,1,0:T(8,128)S(1)}, f32[4,64,...) fusion(f32[27,1,64,256]{3,2,1,0:T(8,128)S(1)} %collective-permu, ...), kind=kLoop, calls=%fused_computation.371 | loop fusion | flops 65536 | bytes 18022400 | tf_op jit(solution)/shard_map/mul | solution.py:94
  70.6 2.5 %fusion.141 = f32[2,4,64,256]{3,2,1,0:T(8,128)S(1)} fusion(f32[2,6,66,258]{3,2,1,0:T(8,128)S(1)} %select_maximum_fusion.16, f32[2,1,64,256]{3,2,1,0:T(8,128)S(1)} %collective-permute-done.3, f32[2,4,64,256]{3,2,1,0:T(8,128)S(1)} %bitcast.125, f32[2,1,64,256]{3,2,1,0:T(8,128)S(1)} %collective-permute-done.2, f32[4,64,256]{2,1,0:T(8,128)S(1)} %get-tuple-element.34, ...), kind=kLoop, calls=%fused_computation.277 | loop fusion | flops 7208960 | bytes 20971520 | tf_op jit(solution)/shard_map/add | solution.py:67
  73.3 3.4 %collective-permute-start.4 = (f32[2,1,64,256]{3,2,1,0:T(8,128)S(1)}, f32[2,1,64,256]{3,2,1,0:T(8,128)S(1)}, u32[]{:S(2)}, u32[]{:S(2)}) collective-permute-start(f32[2,1,64,256]{3,2,1,0:T(8,128)S(1)} %get-tuple-element.82), channel_id=1, source_target_pairs={{0,4},{4,8},{8,12},{1,5},{5,9},{9,13},{2,6},{6,10},{10,14},{3,7},{... | collective-permute-start | bytes 393224 | tf_op jit(solution)/shard_map/ppermute | solution.py:30
  77.9 9.7 %select_maximum_fusion = f32[27,6,66,258]{3,2,1,0:T(8,128)S(1)} fusion(f32[27,1,64,256]{3,2,1,0:T(8,128)} %copy-done.1, f32[27,4,64,256]{3,2,1,0:T(8,128)S(1)} %bitcast.122, f32[27,1,64,256]{3,2,1,0:T(8,128)} %collective-permute-done), kind=kLoop, calls=%fused_computation.5 | loop fusion | flops 41378040 | bytes 21650976 | tf_op jit(solution)/shard_map/concatenate | solution.py:28
  92.6 3.5 %fusion.113 = f32[2,4,64,256]{3,2,1,0:T(8,128)S(1)} fusion(f32[2,6,66,258]{3,2,1,0:T(8,128)S(1)} %select_maximum_fusion.14, f32[2,4,64,256]{3,2,1,0:T(8,128)S(1)} %copy-done.5, f32[2,1,64,256]{3,2,1,0:T(8,128)S(1)} %collective-permute-done.4, f32[2,1,64,256]{3,2,1,0:T(8,128)} %copy-done.113, f32[4,64,256]{2,1,0:T(8,128)S(1)} %copy-done.98, ...), kind=kLoop, calls=%fused_computation.223 | loop fusion | flops 7208960 | bytes 20971520 | tf_op jit(solution)/shard_map/add | solution.py:94
  97.4 4.6 %collective-permute-start.9 = (f32[2,1,64,256]{3,2,1,0:T(8,128)S(1)}, f32[2,1,64,256]{3,2,1,0:T(8,128)S(1)}, u32[]{:S(2)}, u32[]{:S(2)}) collective-permute-start(f32[2,1,64,256]{3,2,1,0:T(8,128)S(1)} %get-tuple-element.80), channel_id=1, source_target_pairs={{0,4},{4,8},{8,12},{1,5},{5,9},{9,13},{2,6},{6,10},{10,14},{3,7},{... | collective-permute-start | bytes 393224 | tf_op jit(solution)/shard_map/ppermute | solution.py:30
  105.9 10.5 %all-reduce.10 = (f32[2]{0:T(128)S(1)}, f32[2]{0:T(128)S(1)}) all-reduce(f32[2]{0:T(128)S(1)} %get-tuple-element.3, f32[2]{0:T(128)S(1)} %get-tuple-element.2), channel_id=1, replica_groups=mesh['groups'=2,'space'=4,'src'=4] {'space'}, use_global_device_ids=true, to_apply=%region_2.3 | all-reduce | flops 4 | bytes 32 | tf_op jit(solution)/shard_map/psum | solution.py:124
  121.3 3.8 %collective-permute-done.11 = f32[2,1,64,256]{3,2,1,0:T(8,128)S(1)} collective-permute-done((f32[2,1,64,256]{3,2,1,0:T(8,128)S(1)}, f32[2,1,64,256]{3,2,1,0:T(8,128)S(1)}, u32[]{:S(2)}, u32[]{:S(2)}) %collective-permute-start.11) | collective-permute-done | bytes 131104 | tf_op jit(solution)/shard_map/ppermute | solution.py:32
  125.8 4.1 %fusion.71 = f32[2,4,64,256]{3,2,1,0:T(8,128)S(1)} fusion(f32[2,6,66,258]{3,2,1,0:T(8,128)S(1)} %select_maximum_fusion.10, f32[2,1,64,256]{3,2,1,0:T(8,128)S(1)} %collective-permute-done.11, f32[2,4,64,256]{3,2,1,0:T(8,128)S(1)} %multiply_subtract_fusion, f32[2,1,64,256]{3,2,1,0:T(8,128)S(1)} %collective-permute-done.10, f32[4,64,256]{2,1,0:T(8,128)S(1)} %copy-done.11, ...), kind=kLoop, calls=%fused_computation.149 | loop fusion | flops 7208960 | bytes 20971520 | tf_op jit(solution)/shard_map/add | solution.py:67
  130.0 2.3 %collective-permute-start.12 = (f32[2,1,64,256]{3,2,1,0:T(8,128)S(1)}, f32[2,1,64,256]{3,2,1,0:T(8,128)S(1)}, u32[]{:S(2)}, u32[]{:S(2)}) collective-permute-start(f32[2,1,64,256]{3,2,1,0:T(8,128)S(1)} %get-tuple-element.76), channel_id=1, source_target_pairs={{0,4},{4,8},{8,12},{1,5},{5,9},{9,13},{2,6},{6,10},{10,14},{3,7},{... | collective-permute-start | bytes 393224 | tf_op jit(solution)/shard_map/ppermute | solution.py:30
  134.2 3.8 %collective-permute-done.13 = f32[2,1,64,256]{3,2,1,0:T(8,128)S(1)} collective-permute-done((f32[2,1,64,256]{3,2,1,0:T(8,128)S(1)}, f32[2,1,64,256]{3,2,1,0:T(8,128)S(1)}, u32[]{:S(2)}, u32[]{:S(2)}) %collective-permute-start.13) | collective-permute-done | bytes 131104 | tf_op jit(solution)/shard_map/ppermute | solution.py:32
  138.7 2.7 %multiply_reduce_fusion = (f32[2]{0:T(128)S(1)}, f32[2,4,64,256]{3,2,1,0:T(8,128)S(1)}) fusion(f32[2,4,64,256]{3,2,1,0:T(8,128)S(1)} %multiply_subtract_fusion, f32[2,6,66,258]{3,2,1,0:T(8,128)S(1)} %select_maximum_fusion.8, f32[4,64,256]{2,1,0:T(8,128)S(1)} %copy-done.99, f32[4,64,256]{2,1,0:T(8,128)S(1)} %copy-done.55, f32[4,64,256]{2,1,0:T(8,128)S(1)} %copy-done.57, ...), kind=kLoop, calls=%fused_computation.332 | loop fusion | flops 7471102 | bytes 21495816 | tf_op jit(solution)/shard_map/reduce_sum | solution.py:120
  141.4 7.5 %psum.30 = f32[2]{0:T(128)S(1)} all-reduce(f32[2]{0:T(128)S(1)} %get-tuple-element.6), channel_id=1, replica_groups=mesh['groups'=2,'space'=4,'src'=4] {'space'}, use_global_device_ids=true, to_apply=%region_6.7 | all-reduce | flops 2 | bytes 16 | tf_op jit(solution)/shard_map/psum | solution.py:124
  150.6 4.0 %collective-permute-start.15 = (f32[2,1,64,256]{3,2,1,0:T(8,128)S(1)}, f32[2,1,64,256]{3,2,1,0:T(8,128)S(1)}, u32[]{:S(2)}, u32[]{:S(2)}) collective-permute-start(f32[2,1,64,256]{3,2,1,0:T(8,128)S(1)} %get-tuple-element.74), channel_id=1, source_target_pairs={{0,4},{4,8},{8,12},{1,5},{5,9},{9,13},{2,6},{6,10},{10,14},{3,7},{... | collective-permute-start | bytes 393224 | tf_op jit(solution)/shard_map/ppermute | solution.py:30
  155.9 4.0 %collective-permute-start.18 = (f32[2,1,64,256]{3,2,1,0:T(8,128)S(1)}, f32[2,1,64,256]{3,2,1,0:T(8,128)S(1)}, u32[]{:S(2)}, u32[]{:S(2)}) collective-permute-start(f32[2,1,64,256]{3,2,1,0:T(8,128)S(1)} %get-tuple-element.70), channel_id=1, source_target_pairs={{0,4},{4,8},{8,12},{1,5},{5,9},{9,13},{2,6},{6,10},{10,14},{3,7},{... | collective-permute-start | bytes 393224 | tf_op jit(solution)/shard_map/ppermute | solution.py:30
  161.4 7.4 %psum.31 = f32[2]{0:T(128)S(1)} all-reduce(f32[2]{0:T(128)S(1)} %fusion.30), channel_id=1, replica_groups=mesh['groups'=2,'space'=4,'src'=4] {'space'}, use_global_device_ids=true, to_apply=%region_8.9 | all-reduce | flops 2 | bytes 16 | tf_op jit(solution)/shard_map/psum | solution.py:174
  170.3 4.0 %collective-permute-start.19 = (f32[2,1,64,256]{3,2,1,0:T(8,128)S(1)}, f32[2,1,64,256]{3,2,1,0:T(8,128)S(1)}, u32[]{:S(2)}, u32[]{:S(2)}) collective-permute-start(f32[2,1,64,256]{3,2,1,0:T(8,128)S(1)} %get-tuple-element.72), channel_id=1, source_target_pairs={{0,4},{4,8},{8,12},{1,5},{5,9},{9,13},{2,6},{6,10},{10,14},{3,7},{... | collective-permute-start | bytes 393224 | tf_op jit(solution)/shard_map/ppermute | solution.py:30
  179.8 35.8 %reduce-scatter.2.cloned.1.call-done = f32[4,16,256]{2,1,0:T(8,128)} async-done(((f32[4,64,256]{2,1,0:T(8,128)}), f32[4,16,256]{2,1,0:T(8,128)}) %reduce-scatter.2.cloned.1.call-update) | async-done | bytes 65552 | tf_op jit(solution)/shard_map/reduce_scatter | solution.py:193
  (312 shorter events, 39.9 us)
Async XLA Ops:
  7.2 15.9 %copy-start.114 = (f32[2,4,64,256]{3,2,1,0:T(8,128)S(1)}, f32[2,4,64,256]{3,2,1,0:T(8,128)}, u32[]{:S(2)}) copy-start(f32[2,4,64,256]{3,2,1,0:T(8,128)} %param.11) | copy-start | bytes 1572868
  7.2 208.4 %reduce-scatter.2.cloned.1.call-start = ((), (), s32[]{:S(2)}) async-start(), calls=%async_computation.1 | async-start | bytes 327680 | tf_op jit(solution)/shard_map/reduce_scatter | solution.py:193
  11.7 52.0 %collective-permute-start.1 = (f32[27,1,64,256]{3,2,1,0:T(8,128)}, f32[27,1,64,256]{3,2,1,0:T(8,128)S(1)}, u32[]{:S(2)}, u32[]{:S(2)}) collective-permute-start(f32[27,1,64,256]{3,2,1,0:T(8,128)} %get-tuple-element.63), channel_id=1, source_target_pairs={{4,0},{8,4},{12,8},{5,1},{9,5},{13,9},{6,2},{10,6},{14,10},{7,3},{... | collective-permute-start | bytes 5308424 | tf_op jit(solution)/shard_map/ppermute | solution.py:32
  13.1 55.2 %collective-permute-start = (f32[27,1,64,256]{3,2,1,0:T(8,128)}, f32[27,1,64,256]{3,2,1,0:T(8,128)}, u32[]{:S(2)}, u32[]{:S(2)}) collective-permute-start(f32[27,1,64,256]{3,2,1,0:T(8,128)} %get-tuple-element.62), channel_id=1, source_target_pairs={{0,4},{4,8},{8,12},{1,5},{5,9},{9,13},{2,6},{6,10},{10,14},{3,7},{... | collective-permute-start | bytes 5308424 | tf_op jit(solution)/shard_map/ppermute | solution.py:30
  19.6 37.1 %collective-permute-start.6 = (f32[1,1,64,256]{3,2,1,0:T(8,128)}, f32[1,1,64,256]{3,2,1,0:T(8,128)S(1)}, u32[]{:S(2)}, u32[]{:S(2)}) collective-permute-start(f32[1,1,64,256]{3,2,1,0:T(8,128)} %get-tuple-element.86), channel_id=1, source_target_pairs={{0,4},{4,8},{8,12},{1,5},{5,9},{9,13},{2,6},{6,10},{10,14},{3,7},{... | collective-permute-start | bytes 196616 | tf_op jit(solution)/shard_map/ppermute | solution.py:30
  21.8 36.3 %collective-permute-start.7 = (f32[1,1,64,256]{3,2,1,0:T(8,128)S(1)}, f32[1,1,64,256]{3,2,1,0:T(8,128)S(1)}, u32[]{:S(2)}, u32[]{:S(2)}) collective-permute-start(f32[1,1,64,256]{3,2,1,0:T(8,128)S(1)} %get-tuple-element.87), channel_id=1, source_target_pairs={{4,0},{8,4},{12,8},{5,1},{9,5},{13,9},{6,2},{10,6},{14,10},{7,3},{... | collective-permute-start | bytes 196616 | tf_op jit(solution)/shard_map/ppermute | solution.py:32
  24.5 35.0 %collective-permute-start.2 = (f32[2,1,64,256]{3,2,1,0:T(8,128)S(1)}, f32[2,1,64,256]{3,2,1,0:T(8,128)S(1)}, u32[]{:S(2)}, u32[]{:S(2)}) collective-permute-start(f32[2,1,64,256]{3,2,1,0:T(8,128)S(1)} %get-tuple-element.84), channel_id=1, source_target_pairs={{0,4},{4,8},{8,12},{1,5},{5,9},{9,13},{2,6},{6,10},{10,14},{3,7},{... | collective-permute-start | bytes 393224 | tf_op jit(solution)/shard_map/ppermute | solution.py:30
  56.8 6.4 %collective-permute-start.3 = (f32[2,1,64,256]{3,2,1,0:T(8,128)S(1)}, f32[2,1,64,256]{3,2,1,0:T(8,128)S(1)}, u32[]{:S(2)}, u32[]{:S(2)}) collective-permute-start(f32[2,1,64,256]{3,2,1,0:T(8,128)S(1)} %get-tuple-element.85), channel_id=1, source_target_pairs={{4,0},{8,4},{12,8},{5,1},{9,5},{13,9},{6,2},{10,6},{14,10},{7,3},{... | collective-permute-start | bytes 393224 | tf_op jit(solution)/shard_map/ppermute | solution.py:32
  73.3 16.9 %collective-permute-start.4 = (f32[2,1,64,256]{3,2,1,0:T(8,128)S(1)}, f32[2,1,64,256]{3,2,1,0:T(8,128)S(1)}, u32[]{:S(2)}, u32[]{:S(2)}) collective-permute-start(f32[2,1,64,256]{3,2,1,0:T(8,128)S(1)} %get-tuple-element.82), channel_id=1, source_target_pairs={{0,4},{4,8},{8,12},{1,5},{5,9},{9,13},{2,6},{6,10},{10,14},{3,7},{... | collective-permute-start | bytes 393224 | tf_op jit(solution)/shard_map/ppermute | solution.py:30
  76.6 13.6 %collective-permute-start.5 = (f32[2,1,64,256]{3,2,1,0:T(8,128)S(1)}, f32[2,1,64,256]{3,2,1,0:T(8,128)S(1)}, u32[]{:S(2)}, u32[]{:S(2)}) collective-permute-start(f32[2,1,64,256]{3,2,1,0:T(8,128)S(1)} %get-tuple-element.83), channel_id=1, source_target_pairs={{4,0},{8,4},{12,8},{5,1},{9,5},{13,9},{6,2},{10,6},{14,10},{7,3},{... | collective-permute-start | bytes 393224 | tf_op jit(solution)/shard_map/ppermute | solution.py:32
  96.1 6.5 %collective-permute-start.8 = (f32[2,1,64,256]{3,2,1,0:T(8,128)S(1)}, f32[2,1,64,256]{3,2,1,0:T(8,128)S(1)}, u32[]{:S(2)}, u32[]{:S(2)}) collective-permute-start(f32[2,1,64,256]{3,2,1,0:T(8,128)S(1)} %get-tuple-element.81), channel_id=1, source_target_pairs={{4,0},{8,4},{12,8},{5,1},{9,5},{13,9},{6,2},{10,6},{14,10},{7,3},{... | collective-permute-start | bytes 393224 | tf_op jit(solution)/shard_map/ppermute | solution.py:32
  97.4 6.6 %collective-permute-start.9 = (f32[2,1,64,256]{3,2,1,0:T(8,128)S(1)}, f32[2,1,64,256]{3,2,1,0:T(8,128)S(1)}, u32[]{:S(2)}, u32[]{:S(2)}) collective-permute-start(f32[2,1,64,256]{3,2,1,0:T(8,128)S(1)} %get-tuple-element.80), channel_id=1, source_target_pairs={{0,4},{4,8},{8,12},{1,5},{5,9},{9,13},{2,6},{6,10},{10,14},{3,7},{... | collective-permute-start | bytes 393224 | tf_op jit(solution)/shard_map/ppermute | solution.py:30
  117.9 3.4 %collective-permute-start.10 = (f32[2,1,64,256]{3,2,1,0:T(8,128)S(1)}, f32[2,1,64,256]{3,2,1,0:T(8,128)S(1)}, u32[]{:S(2)}, u32[]{:S(2)}) collective-permute-start(f32[2,1,64,256]{3,2,1,0:T(8,128)S(1)} %get-tuple-element.78), channel_id=1, source_target_pairs={{0,4},{4,8},{8,12},{1,5},{5,9},{9,13},{2,6},{6,10},{10,14},{3,7},{... | collective-permute-start | bytes 393224 | tf_op jit(solution)/shard_map/ppermute | solution.py:30
  119.3 5.8 %collective-permute-start.11 = (f32[2,1,64,256]{3,2,1,0:T(8,128)S(1)}, f32[2,1,64,256]{3,2,1,0:T(8,128)S(1)}, u32[]{:S(2)}, u32[]{:S(2)}) collective-permute-start(f32[2,1,64,256]{3,2,1,0:T(8,128)S(1)} %get-tuple-element.79), channel_id=1, source_target_pairs={{4,0},{8,4},{12,8},{5,1},{9,5},{13,9},{6,2},{10,6},{14,10},{7,3},{... | collective-permute-start | bytes 393224 | tf_op jit(solution)/shard_map/ppermute | solution.py:32
  125.7 12.8 %copy-start.73 = (f32[4,64,256]{2,1,0:T(8,128)S(1)}, f32[4,64,256]{2,1,0:T(8,128)}, u32[]{:S(2)}) copy-start(f32[4,64,256]{2,1,0:T(8,128)} %copy-done.72) | copy-start | bytes 786436
  130.0 4.2 %collective-permute-start.12 = (f32[2,1,64,256]{3,2,1,0:T(8,128)S(1)}, f32[2,1,64,256]{3,2,1,0:T(8,128)S(1)}, u32[]{:S(2)}, u32[]{:S(2)}) collective-permute-start(f32[2,1,64,256]{3,2,1,0:T(8,128)S(1)} %get-tuple-element.76), channel_id=1, source_target_pairs={{0,4},{4,8},{8,12},{1,5},{5,9},{9,13},{2,6},{6,10},{10,14},{3,7},{... | collective-permute-start | bytes 393224 | tf_op jit(solution)/shard_map/ppermute | solution.py:30
  132.3 5.7 %collective-permute-start.13 = (f32[2,1,64,256]{3,2,1,0:T(8,128)S(1)}, f32[2,1,64,256]{3,2,1,0:T(8,128)S(1)}, u32[]{:S(2)}, u32[]{:S(2)}) collective-permute-start(f32[2,1,64,256]{3,2,1,0:T(8,128)S(1)} %get-tuple-element.77), channel_id=1, source_target_pairs={{4,0},{8,4},{12,8},{5,1},{9,5},{13,9},{6,2},{10,6},{14,10},{7,3},{... | collective-permute-start | bytes 393224 | tf_op jit(solution)/shard_map/ppermute | solution.py:32
  141.4 13.2 %copy-start.7 = (f32[2,4,64,256]{3,2,1,0:T(8,128)S(1)}, f32[2,4,64,256]{3,2,1,0:T(8,128)}, u32[]{:S(2)}) copy-start(f32[2,4,64,256]{3,2,1,0:T(8,128)} %param.10) | copy-start | bytes 1572868
  149.2 10.8 %collective-permute-start.14 = (f32[2,1,64,256]{3,2,1,0:T(8,128)S(1)}, f32[2,1,64,256]{3,2,1,0:T(8,128)S(1)}, u32[]{:S(2)}, u32[]{:S(2)}) collective-permute-start(f32[2,1,64,256]{3,2,1,0:T(8,128)S(1)} %get-tuple-element.75), channel_id=1, source_target_pairs={{4,0},{8,4},{12,8},{5,1},{9,5},{13,9},{6,2},{10,6},{14,10},{7,3},{... | collective-permute-start | bytes 393224 | tf_op jit(solution)/shard_map/ppermute | solution.py:32
  150.6 9.4 %collective-permute-start.15 = (f32[2,1,64,256]{3,2,1,0:T(8,128)S(1)}, f32[2,1,64,256]{3,2,1,0:T(8,128)S(1)}, u32[]{:S(2)}, u32[]{:S(2)}) collective-permute-start(f32[2,1,64,256]{3,2,1,0:T(8,128)S(1)} %get-tuple-element.74), channel_id=1, source_target_pairs={{0,4},{4,8},{8,12},{1,5},{5,9},{9,13},{2,6},{6,10},{10,14},{3,7},{... | collective-permute-start | bytes 393224 | tf_op jit(solution)/shard_map/ppermute | solution.py:30
  154.6 19.6 %collective-permute-start.16 = (f32[2,1,64,256]{3,2,1,0:T(8,128)S(1)}, f32[2,1,64,256]{3,2,1,0:T(8,128)S(1)}, u32[]{:S(2)}, u32[]{:S(2)}) collective-permute-start(f32[2,1,64,256]{3,2,1,0:T(8,128)S(1)} %get-tuple-element.71), channel_id=1, source_target_pairs={{4,0},{8,4},{12,8},{5,1},{9,5},{13,9},{6,2},{10,6},{14,10},{7,3},{... | collective-permute-start | bytes 393224 | tf_op jit(solution)/shard_map/ppermute | solution.py:32
  155.9 18.3 %collective-permute-start.18 = (f32[2,1,64,256]{3,2,1,0:T(8,128)S(1)}, f32[2,1,64,256]{3,2,1,0:T(8,128)S(1)}, u32[]{:S(2)}, u32[]{:S(2)}) collective-permute-start(f32[2,1,64,256]{3,2,1,0:T(8,128)S(1)} %get-tuple-element.70), channel_id=1, source_target_pairs={{0,4},{4,8},{8,12},{1,5},{5,9},{9,13},{2,6},{6,10},{10,14},{3,7},{... | collective-permute-start | bytes 393224 | tf_op jit(solution)/shard_map/ppermute | solution.py:30
  169.0 6.8 %collective-permute-start.17 = (f32[2,1,64,256]{3,2,1,0:T(8,128)S(1)}, f32[2,1,64,256]{3,2,1,0:T(8,128)S(1)}, u32[]{:S(2)}, u32[]{:S(2)}) collective-permute-start(f32[2,1,64,256]{3,2,1,0:T(8,128)S(1)} %get-tuple-element.73), channel_id=1, source_target_pairs={{4,0},{8,4},{12,8},{5,1},{9,5},{13,9},{6,2},{10,6},{14,10},{7,3},{... | collective-permute-start | bytes 393224 | tf_op jit(solution)/shard_map/ppermute | solution.py:32
  170.3 7.3 %collective-permute-start.19 = (f32[2,1,64,256]{3,2,1,0:T(8,128)S(1)}, f32[2,1,64,256]{3,2,1,0:T(8,128)S(1)}, u32[]{:S(2)}, u32[]{:S(2)}) collective-permute-start(f32[2,1,64,256]{3,2,1,0:T(8,128)S(1)} %get-tuple-element.72), channel_id=1, source_target_pairs={{0,4},{4,8},{8,12},{1,5},{5,9},{9,13},{2,6},{6,10},{10,14},{3,7},{... | collective-permute-start | bytes 393224 | tf_op jit(solution)/shard_map/ppermute | solution.py:30
  (118 other events, 679.6 us)
Sparse Core Ops, SparseCore 0:
  179.9 35.6 reduce-scatter.1
where the time goes:
time: 224 us; the launch traced here: 222 us
  waiting for transfers between devices  81.1 us (36%)
  starting transfers between devices  49.1 us (22%)
  other arithmetic  40.2 us (18%)
  blocking collectives  25.4 us (11%)
  between operations  16.1 us (7%)
  local copies, waits for them, and re-layouts  10.6 us (5%)
    reduce_scatter x1, waiting for transfers between devices, body(): lax.psum_scatter(local_term, 'src', scatter_dimension=1, tiled=True)  35.8 us
    ppermute x10, starting transfers between devices, extended(): lax.ppermute(tail, axis, [(i, (i + 1) % count) for i in range(ends)])  35.7 us
    ppermute x10, waiting for transfers between devices, extended(): lax.ppermute(tail, axis, [(i, (i + 1) % count) for i in range(ends)])  32.8 us
    psum x2, blocking collectives, aligned_total(): return lax.psum(local_sums(residual, smoothed), 'space')  18 us
    ppermute x10, starting transfers between devices, extended(): lax.ppermute(head, axis, [((i + 1) % count, i) for i in range(ends)])  13.3 us
    concatenate x9, other arithmetic, extended(): jnp.concatenate([lax.ppermute(tail, axis, [(i, (i + 1) % count) for i in...  13.1 us
    ppermute x10, waiting for transfers between devices, extended(): lax.ppermute(head, axis, [((i + 1) % count, i) for i in range(ends)])  12.4 us
    psum x1, blocking collectives, body(): lax.psum(local_sums(direction, image_field), 'space')  7.39 us
  transfers between devices with their start and end apart: 21, of which 11 were waited for; matrix products, arithmetic and copies ran while one was open for 10% of the time, Pallas kernels for 0%

commit v1 on v0

v1 whole, which is shorter than its diff:
```python
import functools

import jax
import jax.numpy as jnp
from jax import lax
from jax.experimental import pallas as pl
from jax.experimental.pallas import tpu as pltpu
from jax.sharding import PartitionSpec as P

ITERS = 2
MASS = 0.05
CURRENT = 5.0
PAD = 8
ROWS = 8
LANES = 128
CHUNKS = 9
MESH = pl.DeviceIdType.MESH


def kernel(
    dims,
    elec,
    assign,
    lines,
    sigma_hbm,
    coef_hbm,
    fwd_hbm,
    misfit_hbm,
    adj_hbm,
    grad_hbm,
    coef,
    sig,
    weights,
    res,
    dirn,
    fwd,
    adj,
    quart,
    part,
    from_left,
    from_right,
    image,
    img_left,
    img_right,
    gsum,
    grecv,
    gout,
    psend,
    precv,
    local_sem,
    out_sem,
    halo_send,
    halo_recv,
    sum_send,
    sum_recv,
    grad_send,
    grad_recv,
):
    n, nsrc, S, X, H, Z = dims
    me = lax.axis_index("space")
    mine = lax.axis_index("src")
    has_left, has_right = me > 0, me < n - 1
    left, right = lax.rem(me + n - 1, n), lax.rem(me + 1, n)
    tiles = H // ROWS
    inner = pl.ds(PAD, H)

    def plain(j):
        return pl.ds(pl.multiple_of(ROWS * j, ROWS), ROWS)

    def padded(j):
        return pl.ds(pl.multiple_of(PAD + ROWS * j, ROWS), ROWS)

    lane = lax.broadcasted_iota(jnp.int32, (ROWS, Z), 1)
    line = lax.broadcasted_iota(jnp.int32, (ROWS, Z), 0)

    def beside(ref, at, j, b):
        here = ref[(*at, padded(j), slice(None))]
        if b == 0:
            return here
        other = ref[(*at, padded(j + b), slice(None))]
        if b == 1:
            return pltpu.roll(jnp.where(line == 0, other, here), ROWS - 1, 0)
        return pltpu.roll(jnp.where(line == ROWS - 1, other, here), 1, 0)

    def along(v, c):
        if c == 0:
            return v
        if c == 1:
            return jnp.where(lane == Z - 1, 0.0, pltpu.roll(v, Z - 1, 1))
        return jnp.where(lane == 0, 0.0, pltpu.roll(v, 1, 1))

    class Halo:
        def __init__(self, slot, to_left, left_dst, to_right, right_dst):
            self.go_left = pltpu.make_async_remote_copy(
                to_left, left_dst, halo_send.at[slot, 0], halo_recv.at[slot, 0],
                device_id={"space": left}, device_id_type=MESH)
            self.go_right = pltpu.make_async_remote_copy(
                to_right, right_dst, halo_send.at[slot, 1], halo_recv.at[slot, 1],
                device_id={"space": right}, device_id_type=MESH)

        def start(self):
            pl.when(has_left)(self.go_left.start)
            pl.when(has_right)(self.go_right.start)

        def arrive(self):
            pl.when(has_right)(self.go_left.wait_recv)
            pl.when(has_left)(self.go_right.wait_recv)

        def leave(self):
            pl.when(has_left)(self.go_left.wait_send)
            pl.when(has_right)(self.go_right.wait_send)

    load_misfit = [
        pltpu.make_async_copy(misfit_hbm.at[s], res.at[s, pl.ds(1, X), inner, :], local_sem.at[s])
        for s in range(S)
    ]
    load_fwd = [
        pltpu.make_async_copy(fwd_hbm.at[s], fwd.at[s, pl.ds(1, X), inner, :], local_sem.at[S + s])
        for s in range(S)
    ]
    load_sigma = pltpu.make_async_copy(
        sigma_hbm, sig.at[pl.ds(1, X), inner, :], local_sem.at[2 * S])
    group = 27 // CHUNKS
    load_coef = [
        pltpu.make_async_copy(
            coef_hbm.at[pl.ds(group * i, group)], coef.at[pl.ds(group * i, group)],
            local_sem.at[2 * S + 1 + i])
        for i in range(CHUNKS)
    ]
    for copy in load_misfit:
        copy.start()
    for copy in load_coef:
        copy.start()
    load_sigma.start()
    for copy in load_fwd:
        copy.start()

    barrier = pltpu.get_barrier_semaphore()
    for k in range(1, n):
        pl.semaphore_signal(
            barrier, inc=1, device_id={"space": lax.rem(me + k, n)}, device_id_type=MESH)
    for k in range(1, nsrc):
        pl.semaphore_signal(
            barrier, inc=1, device_id={"src": lax.rem(mine + k, nsrc)}, device_id_type=MESH)

    for ref in (res, dirn, fwd, adj):
        edge = jnp.zeros((S, X + 2, PAD, Z), jnp.float32)
        ref[:, :, pl.ds(0, PAD), :] = edge
        ref[:, :, pl.ds(PAD + H, PAD), :] = edge
    edge = jnp.zeros((X + 2, PAD, Z), jnp.float32)
    sig[:, pl.ds(0, PAD), :] = edge
    sig[:, pl.ds(PAD + H, PAD), :] = edge
    for b in range(3):
        quart[b, :, pl.ds(0, PAD), :] = edge
        quart[b, :, pl.ds(PAD + H, PAD), :] = edge

    def clear(p):
        plane = jnp.zeros((S, H, Z), jnp.float32)
        res[:, p, inner, :] = plane
        fwd[:, p, inner, :] = plane
        sig[p, inner, :] = jnp.zeros((H, Z), jnp.float32)

    pl.when(jnp.logical_not(has_left))(lambda: clear(0))
    pl.when(jnp.logical_not(has_right))(lambda: clear(X + 1))

    pl.semaphore_wait(barrier, n - 1 + nsrc - 1)

    res_halo = [
        Halo(s, res.at[s, 1, inner, :], res.at[s, X + 1, inner, :],
             res.at[s, X, inner, :], res.at[s, 0, inner, :])
        for s in range(S)
    ]
    part_halo = [
        [
            Halo(S + it * S + s, part.at[s, pl.ds(0, 2)], from_right.at[it, s],
                 part.at[s, pl.ds(X, 2)], from_left.at[it, s])
            for s in range(S)
        ]
        for it in range(2)
    ]
    img_halo = [
        Halo(3 * S + s, image.at[s, 0], img_right.at[s], image.at[s, X - 1], img_left.at[s])
        for s in range(S)
    ]
    fwd_halo = [
        Halo(4 * S + s, fwd_hbm.at[s, 0], fwd.at[s, X + 1, inner, :],
             fwd_hbm.at[s, X - 1], fwd.at[s, 0, inner, :])
        for s in range(S)
    ]
    sig_halo = Halo(5 * S, sigma_hbm.at[0], sig.at[X + 1, inner, :],
                    sigma_hbm.at[X - 1], sig.at[0, inner, :])

    def fold(t):
        total = t[:, :LANES]
        for i in range(1, Z // LANES):
            total = total + t[:, LANES * i : LANES * (i + 1)]
        return total

    def sum_copies(slot):
        return [
            pltpu.make_async_remote_copy(
                psend.at[slot], precv.at[slot, k], sum_send.at[slot, k], sum_recv.at[slot, k],
                device_id={"space": lax.rem(me + k, n)}, device_id_type=MESH)
            for k in range(1, n)
        ]

    def sum_start(slot, t):
        psend[slot] = fold(t)
        for copy in sum_copies(slot):
            copy.start()

    def sum_finish(slot):
        total = psend[slot]
        for k, copy in enumerate(sum_copies(slot)):
            copy.wait()
            total = total + precv[slot, k + 1]
        return jnp.sum(total, keepdims=True)

    def precondition(s):
        def step(j, squares):
            sums = [jnp.zeros((ROWS, Z), jnp.float32) for _ in range(X)]
            for p in range(X + 2):
                for b in (-1, 0, 1):
                    v = beside(res, (s, p), j, b)
                    for c in (-1, 0, 1):
                        vc = along(v, c)
                        for a in (-1, 0, 1):
                            x = p - 1 - a
                            if 0 <= x < X:
                                k = 9 * (a + 1) + 3 * (b + 1) + c + 1
                                sums[x] = sums[x] + coef[k, x, plain(j), :] * vc
            for x in range(X):
                squares = squares + sums[x] * sums[x]
            for p in range(X + 2):
                for b in (-1, 0, 1):
                    total = None
                    for c in (-1, 0, 1):
                        given = None
                        for a in (-1, 0, 1):
                            x = p - 1 - a
                            if 0 <= x < X:
                                k = 9 * (a + 1) + 3 * (b + 1) + c + 1
                                term = coef[k, x, plain(j), :] * sums[x]
                                given = term if given is None else given + term
                        given = along(given, -c)
                        total = given if total is None else total + given
                    quart[b + 1, p, padded(j), :] = total
            return squares

        squares = lax.fori_loop(0, tiles, step, jnp.zeros((ROWS, Z), jnp.float32))

        def gather(j, carry):
            for p in range(X + 2):
                part[s, p, plain(j), :] = (
                    quart[1, p, padded(j), :] + beside(quart, (2, p), j, -1)
                    + beside(quart, (0, p), j, 1))
            return carry

        lax.fori_loop(0, tiles, gather, 0)
        return squares

    def find_weights():
        def step(j, carry):
            for x in range(X):
                here = sig[x + 1, padded(j), :]
                sides = (
                    sig[x + 2, padded(j), :], sig[x, padded(j), :],
                    beside(sig, (x + 1,), j, 1), beside(sig, (x + 1,), j, -1),
                    along(here, 1), along(here, -1))
                diagonal = jnp.full((ROWS, Z), MASS, jnp.float32)
                for i, side in enumerate(sides):
                    w = 0.5 * (here + side)
                    weights[i, x, plain(j), :] = w
                    diagonal = diagonal + w
                weights[6, x, plain(j), :] = diagonal
            return carry

        lax.fori_loop(0, tiles, step, 0)

    def operate(s, planes, sofar):
        def step(j, dots):
            for x in planes:
                d = dirn[s, x + 1, padded(j), :]
                sides = (
                    dirn[s, x + 2, padded(j), :], dirn[s, x, padded(j), :],
                    beside(dirn, (s, x + 1), j, 1), beside(dirn, (s, x + 1), j, -1),
                    along(d, 1), along(d, -1))
                out = weights[6, x, plain(j), :] * d
                for i, side in enumerate(sides):
                    out = out - weights[i, x, plain(j), :] * side
                image[s, x, plain(j), :] = out
                dots = dots + d * out
            return dots

        return lax.fori_loop(0, tiles, step, sofar)

    def set_direction(s, it, growth):
        def step(j, carry):
            for p in range(X + 2):
                d = part[s, p, plain(j), :]
                if p < 2:
                    d = d + jnp.where(has_left, from_left[it, s, p, plain(j), :], 0.0)
                if p >= X:
                    d = d + jnp.where(has_right, from_right[it, s, p - X, plain(j), :], 0.0)
                if p == 0:
                    d = jnp.where(has_left, d, 0.0)
                if p == X + 1:
                    d = jnp.where(has_right, d, 0.0)
                if growth is not None:
                    d = d + growth * dirn[s, p, padded(j), :]
                dirn[s, p, padded(j), :] = d
            return carry

        lax.fori_loop(0, tiles, step, 0)

    def add_step(s, size, first):
        def step(j, carry):
            for p in range(X + 2):
                v = size * dirn[s, p, padded(j), :]
                if not first:
                    v = v + adj[s, p, padded(j), :]
                adj[s, p, padded(j), :] = v
            return carry

        lax.fori_loop(0, tiles, step, 0)

    def drop_step(s, size):
        def step(j, carry):
            for x in range(X):
                res[s, x + 1, padded(j), :] = (
                    res[s, x + 1, padded(j), :] - size * image[s, x, plain(j), :])
            res[s, 0, padded(j), :] = res[s, 0, padded(j), :] - jnp.where(
                has_left, size * img_left[s, plain(j), :], 0.0)
            res[s, X + 1, padded(j), :] = res[s, X + 1, padded(j), :] - jnp.where(
                has_right, size * img_right[s, plain(j), :], 0.0)
            return carry

        lax.fori_loop(0, tiles, step, 0)

    def add_electrodes(s):
        at = lax.broadcasted_iota(jnp.int32, (ROWS, Z), 0) * Z + lane
        plus = elec[s, 0] - me * (X * H * Z)
        minus = elec[s, 1] - me * (X * H * Z)

        def step(j, carry):
            for x in range(X):
                here = at + (x * H + ROWS * j) * Z
                v = res[s, x + 1, padded(j), :]
                v = v + jnp.where(here == plus, CURRENT, 0.0)
                v = v - jnp.where(here == minus, CURRENT, 0.0)
                res[s, x + 1, padded(j), :] = v
            return carry

        lax.fori_loop(0, tiles, step, 0)

    zero = jnp.zeros((ROWS, Z), jnp.float32)
    for s in range(S):
        load_misfit[s].wait()
        add_electrodes(s)
        res_halo[s].start()
    sig_halo.start()
    for copy in load_coef:
        copy.wait()

    for s in range(S):
        res_halo[s].arrive()
        squares = precondition(s)
        part_halo[0][s].start()
        sum_start(s, squares)

    load_sigma.wait()
    sig_halo.arrive()
    find_weights()

    for s in range(S):
        part_halo[0][s].arrive()
        set_direction(s, 0, None)
        dots = operate(s, (0, X - 1), zero)
        img_halo[s].start()
        dots = operate(s, tuple(range(1, X - 1)), dots)
        sum_start(S + s, dots)
    for s in range(S):
        fwd_halo[s].start()

    align = []
    for s in range(S):
        align.append(sum_finish(s))
        size = align[s] / sum_finish(S + s)
        add_step(s, size, True)
        img_halo[s].arrive()
        res_halo[s].leave()
        drop_step(s, size)
        part_halo[0][s].leave()
        squares = precondition(s)
        part_halo[1][s].start()
        sum_start(2 * S + s, squares)

    for s in range(S):
        part_halo[1][s].arrive()
        now = sum_finish(2 * S + s)
        set_direction(s, 1, now / align[s])
        align[s] = now
        img_halo[s].leave()
        dots = operate(s, tuple(range(X)), zero)
        sum_start(3 * S + s, dots)

    save = []
    for s in range(S):
        size = align[s] / sum_finish(3 * S + s)
        add_step(s, size, False)
        save.append(pltpu.make_async_copy(
            adj.at[s, pl.ds(1, X), inner, :], adj_hbm.at[s], out_sem.at[s]))
        save[s].start()
    for s in range(S):
        load_fwd[s].wait()
        fwd_halo[s].arrive()

    scale = []
    for s in range(S):
        w = jnp.float32(0.0)
        for i in range(lines.shape[0]):
            w = w + jnp.where(assign[s] == i, lines[i], 0.0)
        scale.append(-0.5 * w)

    def gradient(j, carry):
        for x in range(X):
            total = None
            for s in range(S):
                f, a = fwd[s, x + 1, padded(j), :], adj[s, x + 1, padded(j), :]
                sides = [
                    (r[s, x + 2, padded(j), :], r[s, x, padded(j), :],
                     beside(r, (s, x + 1), j, 1), beside(r, (s, x + 1), j, -1),
                     along(v, 1), along(v, -1))
                    for r, v in ((fwd, f), (adj, a))
                ]
                sums = None
                for fs, as_ in zip(*sides):
                    term = (f - fs) * (a - as_)
                    sums = term if sums is None else sums + term
                term = scale[s] * sums
                total = term if total is None else total + term
            gsum[x, plain(j), :] = total
        return carry

    lax.fori_loop(0, tiles, gradient, 0)

    count = H // nsrc

    def share(t):
        return pl.ds(pl.multiple_of(count * t, count), count)

    give = []
    for k in range(1, nsrc):
        to = lax.rem(mine + k, nsrc)
        give.append(pltpu.make_async_remote_copy(
            gsum.at[:, share(to), :], grecv.at[k - 1], grad_send.at[k], grad_recv.at[k],
            device_id={"src": to}, device_id_type=MESH))
        give[-1].start()
    total = gsum[:, share(mine), :]
    for k in range(1, nsrc):
        give[k - 1].wait()
        total = total + grecv[k - 1]
    gout[...] = total
    last = pltpu.make_async_copy(gout, grad_hbm, out_sem.at[S])
    last.start()

    for s in range(S):
        part_halo[1][s].leave()
        fwd_halo[s].leave()
        save[s].wait()
    sig_halo.leave()
    last.wait()


def body(n, nsrc, conductivity, inverse_coefficients, forward_potential, misfit_field,
         electrodes, assignment, line_weight):
    S, X, H, Z = misfit_field.shape
    f32 = jnp.float32
    tall = H + 2 * PAD
    field = pltpu.VMEM((S, X + 2, tall, Z), f32)
    dma = pltpu.SemaphoreType.DMA
    smem = pl.BlockSpec(memory_space=pltpu.SMEM)
    anywhere = pl.BlockSpec(memory_space=pl.ANY)
    return pl.pallas_call(
        functools.partial(kernel, (n, nsrc, S, X, H, Z)),
        out_shape=(
            jax.ShapeDtypeStruct((S, X, H, Z), f32),
            jax.ShapeDtypeStruct((X, H // nsrc, Z), f32),
        ),
        in_specs=[smem] * 3 + [anywhere] * 4,
        out_specs=(anywhere, anywhere),
        scratch_shapes=[
            pltpu.VMEM((27, X, H, Z), f32),
            pltpu.VMEM((X + 2, tall, Z), f32),
            pltpu.VMEM((7, X, H, Z), f32),
            field, field, field, field,
            pltpu.VMEM((3, X + 2, tall, Z), f32),
            pltpu.VMEM((S, X + 2, H, Z), f32),
            pltpu.VMEM((ITERS, S, 2, H, Z), f32),
            pltpu.VMEM((ITERS, S, 2, H, Z), f32),
            pltpu.VMEM((S, X, H, Z), f32),
            pltpu.VMEM((S, H, Z), f32),
            pltpu.VMEM((S, H, Z), f32),
            pltpu.VMEM((X, H, Z), f32),
            pltpu.VMEM((nsrc - 1, X, H // nsrc, Z), f32),
            pltpu.VMEM((X, H // nsrc, Z), f32),
            pltpu.VMEM((4 * S, ROWS, LANES), f32),
            pltpu.VMEM((4 * S, n, ROWS, LANES), f32),
            dma((2 * S + 1 + CHUNKS,)),
            dma((S + 1,)),
            dma((5 * S + 1, 2)),
            dma((5 * S + 1, 2)),
            dma((4 * S, n)),
            dma((4 * S, n)),
            dma((nsrc,)),
            dma((nsrc,)),
        ],
        compiler_params=pltpu.CompilerParams(
            collective_id=0, has_side_effects=True, vmem_limit_bytes=60 * 1024 * 1024),
    )(electrodes, assignment, line_weight, conductivity, inverse_coefficients,
      forward_potential, misfit_field)


def solution(mesh):
    in_specs = (
        P(("groups", "space"), None, None),
        P(None, ("groups", "space"), None, None),
        P(("groups", "src"), "space", None, None),
        P(("groups", "src"), "space", None, None),
        P(("groups", "src"), None),
        P(("groups", "src")),
        P("groups"),
    )
    out_specs = (P(("groups", "src"), "space", None, None), P(("groups", "space"), "src", None))
    run = functools.partial(body, mesh.shape["space"], mesh.shape["src"])
    return jax.shard_map(run, mesh=mesh, in_specs=in_specs, out_specs=out_specs, check_vma=False)
```

time: 224 us -> 49.1 us (0.22)
  waiting for transfers between devices: 81.1 us -> 0 us
  starting transfers between devices: 49.1 us -> 0 us
  Pallas kernels: 0 us -> 44.9 us
  other arithmetic: 40.2 us -> 0 us
  blocking collectives: 25.4 us -> 0 us
  between operations: 16.1 us -> 0.64 us
  local copies, waits for them, and re-layouts: 10.6 us -> 3.34 us
    ppermute x20 -> x0, starting transfers between devices: 49 us -> none  [the longest x10 35.7 us: extended(): lax.ppermute(tail, axis, [(i, (i + 1) % count) for i in range(ends)])]
    ppermute x20 -> x0, waiting for transfers between devices: 45.2 us -> none  [the longest x10 32.8 us: extended(): lax.ppermute(tail, axis, [(i, (i + 1) % count) for i in range(ends)])]
    pallas_call x0 -> x1, Pallas kernels: none -> 44.9 us  [body(): pl.pallas_call(functools.partial(kernel, (n, nsrc, S, X, H, Z)), out_shap...]
    reduce_scatter x1 -> x0, waiting for transfers between devices: 35.8 us -> none  [body(): lax.psum_scatter(local_term, 'src', scatter_dimension=1, tiled=True)]
    psum x3 -> x0, blocking collectives: 25.4 us -> none  [the longest x2 18 us: aligned_total(): return lax.psum(local_sums(residual, smoothed), 'space')]
    concatenate x10 -> x0, other arithmetic: 13.1 us -> none  [the longest x9 13.1 us: extended(): jnp.concatenate([lax.ppermute(tail, axis, [(i, (i + 1) % count) for i in...]
    add x5 -> x0, other arithmetic: 10.3 us -> none  [the longest x2 6.56 us: apply_forward(): accumulated + coef_slab[position] * padded[:, 1 + step_x:1 + step_x + sla...]
    mul x4 -> x0, other arithmetic: 7.6 us -> none  [the longest x2 6.38 us: apply_transposed(): accumulated = accumulated + coef_part * field_part]
  transfers between devices with their start and end apart: 21 -> 0, of which waited for: 11 -> 0; matrix products, arithmetic and copies ran while one was open for 10% -> 0% of each run, Pallas kernels for 0% -> 0%
where the time goes in v1:
time: 49.1 us; the launch traced here: 48.9 us
  Pallas kernels  44.9 us (91%)
  local copies, waits for them, and re-layouts  3.34 us (7%)
  between operations  0.64 us (1%)
    pallas_call x1, Pallas kernels, body(): pl.pallas_call(functools.partial(kernel, (n, nsrc, S, X, H, Z)), out_shap...  44.9 us
    unnamed x2, local copies, waits for them, and re-layouts  3.34 us

profile of v1, /device:TPU:1, one launch (start us, length us, event | category | flops | bytes accessed | tf_op | source)
XLA Modules:
  0.0 48.9 jit_solution(2598480022520965768)
XLA Ops:
  0.6 44.9 %shard_map.86 = (f32[2,4,64,256]{3,2,1,0:T(8,128)}, f32[4,16,256]{2,1,0:T(8,128)}) custom-call(s32[2,2]{1,0:T(2,128)} %elec.1, s32[2]{0:T(128)} %assign.1, f32[4]{0:T(128)} %lines.1, f32[4,64,256]{2,1,0:T(8,128)} %sigma_hbm.1, f32[27,4,64,256]{3,2,1,0:T(8,128)} %coef_hbm.1, f32[2,4,64,256]{3,2,1,0:T(8,128)} %fwd_hbm.1, f32[2,4,64,256]{3,2,1,0:T(8,128)} %misfit_hbm.1), custom_call_target="tpu_custom_call" | custom-call | tf_op jit(solution)/shard_map/pallas_call | solution.py:484
  45.5 1.9 %copy.11 = f32[2,4,64,256]{3,2,1,0:T(8,128)} copy(f32[2,4,64,256]{3,2,1,0:T(8,128)} %get-tuple-element.4) | data formatting | bytes 1048576
  47.4 1.5 %copy.12 = f32[4,16,256]{2,1,0:T(8,128)} copy(f32[4,16,256]{2,1,0:T(8,128)} %get-tuple-element.5) | data formatting | bytes 131072

commit v2 on v1

v2 whole, which is shorter than its diff:
```python
import functools

import jax
import jax.numpy as jnp
from jax import lax
from jax.experimental import pallas as pl
from jax.experimental.pallas import tpu as pltpu
from jax.sharding import PartitionSpec as P

ITERS = 2
MASS = 0.05
CURRENT = 5.0
PAD = 8
ROWS = 8
LANES = 128
CHUNKS = 9
MESH = pl.DeviceIdType.MESH


def kernel(
    dims,
    elec,
    assign,
    lines,
    sigma_hbm,
    coef_hbm,
    fwd_hbm,
    misfit_hbm,
    adj_hbm,
    grad_hbm,
    coef,
    sig,
    weights,
    res,
    fwd,
    img,
    next_dir,
    first_dir,
    smooth,
    quart,
    part,
    from_left,
    from_right,
    gsum,
    gpart,
    out,
    grecv,
    gout,
    psend,
    precv,
    local_sem,
    out_sem,
    halo_send,
    halo_recv,
    sum_send,
    sum_recv,
    grad_send,
    grad_recv,
):
    n, nsrc, S, X, H, Z = dims
    me = lax.axis_index("space")
    mine = lax.axis_index("src")
    has_left, has_right = me > 0, me < n - 1
    left, right = lax.rem(me + n - 1, n), lax.rem(me + 1, n)
    tiles = H // ROWS
    inner = pl.ds(PAD, H)

    def plain(j):
        return pl.ds(pl.multiple_of(ROWS * j, ROWS), ROWS)

    def padded(j):
        return pl.ds(pl.multiple_of(PAD + ROWS * j, ROWS), ROWS)

    lane = lax.broadcasted_iota(jnp.int32, (ROWS, Z), 1)
    zero = jnp.zeros((ROWS, Z), jnp.float32)
    line = lax.broadcasted_iota(jnp.int32, (ROWS, Z), 0)

    def beside(ref, at, j, b):
        here = ref[(*at, padded(j), slice(None))]
        if b == 0:
            return here
        other = ref[(*at, padded(j + b), slice(None))]
        if b == 1:
            return pltpu.roll(jnp.where(line == 0, other, here), ROWS - 1, 0)
        return pltpu.roll(jnp.where(line == ROWS - 1, other, here), 1, 0)

    def along(v, c):
        if c == 0:
            return v
        if c == 1:
            return jnp.where(lane == Z - 1, 0.0, pltpu.roll(v, Z - 1, 1))
        return jnp.where(lane == 0, 0.0, pltpu.roll(v, 1, 1))

    class Halo:
        def __init__(self, slot, to_left, left_dst, to_right, right_dst):
            self.go_left = pltpu.make_async_remote_copy(
                to_left, left_dst, halo_send.at[slot, 0], halo_recv.at[slot, 0],
                device_id={"space": left}, device_id_type=MESH)
            self.go_right = pltpu.make_async_remote_copy(
                to_right, right_dst, halo_send.at[slot, 1], halo_recv.at[slot, 1],
                device_id={"space": right}, device_id_type=MESH)

        def start(self):
            pl.when(has_left)(self.go_left.start)
            pl.when(has_right)(self.go_right.start)

        def arrive(self):
            pl.when(has_right)(self.go_left.wait_recv)
            pl.when(has_left)(self.go_right.wait_recv)

        def leave(self):
            pl.when(has_left)(self.go_left.wait_send)
            pl.when(has_right)(self.go_right.wait_send)

    load_misfit = [
        pltpu.make_async_copy(misfit_hbm.at[s], res.at[s, pl.ds(1, X), inner, :], local_sem.at[s])
        for s in range(S)
    ]
    load_fwd = [
        pltpu.make_async_copy(fwd_hbm.at[s], fwd.at[s, pl.ds(1, X), inner, :], local_sem.at[S + s])
        for s in range(S)
    ]
    load_sigma = pltpu.make_async_copy(
        sigma_hbm, sig.at[pl.ds(2, X), inner, :], local_sem.at[2 * S])
    group = 27 // CHUNKS
    load_coef = [
        pltpu.make_async_copy(
            coef_hbm.at[pl.ds(group * i, group)], coef.at[pl.ds(group * i, group)],
            local_sem.at[2 * S + 1 + i])
        for i in range(CHUNKS)
    ]
    for copy in load_misfit:
        copy.start()
    for copy in load_coef:
        copy.start()
    load_sigma.start()
    for copy in load_fwd:
        copy.start()

    barrier = pltpu.get_barrier_semaphore()
    for k in range(1, n):
        pl.semaphore_signal(
            barrier, inc=1, device_id={"space": lax.rem(me + k, n)}, device_id_type=MESH)
    for k in range(1, nsrc):
        pl.semaphore_signal(
            barrier, inc=1, device_id={"src": lax.rem(mine + k, nsrc)}, device_id_type=MESH)

    def clear_rows(ref):
        planes = ref.shape[0]
        edge = jnp.zeros((planes, PAD, Z), jnp.float32)
        ref[:, pl.ds(0, PAD), :] = edge
        ref[:, pl.ds(PAD + H, PAD), :] = edge

    for s in range(S):
        for ref in (res, fwd, img, next_dir, first_dir):
            clear_rows(ref.at[s])
    clear_rows(sig)
    for b in range(3):
        clear_rows(quart.at[b])

    def clear(p, q):
        plane = jnp.zeros((S, H, Z), jnp.float32)
        res[:, p, inner, :] = plane
        fwd[:, p, inner, :] = plane
        sig[pl.ds(q, 2), inner, :] = jnp.zeros((2, H, Z), jnp.float32)

    pl.when(jnp.logical_not(has_left))(lambda: clear(0, 0))
    pl.when(jnp.logical_not(has_right))(lambda: clear(X + 1, X + 2))

    pl.semaphore_wait(barrier, n - 1 + nsrc - 1)

    res_halo = [
        Halo(s, res.at[s, 1, inner, :], res.at[s, X + 1, inner, :],
             res.at[s, X, inner, :], res.at[s, 0, inner, :])
        for s in range(S)
    ]
    part_halo = [
        [
            Halo(S + s, part.at[0, s, pl.ds(0, 3)], from_right.at[0, s],
                 part.at[0, s, pl.ds(X - 1, 3)], from_left.at[0, s])
            for s in range(S)
        ],
        [
            Halo(2 * S + s, part.at[1, s, pl.ds(0, 2)], from_right.at[1, s, pl.ds(0, 2)],
                 part.at[1, s, pl.ds(X, 2)], from_left.at[1, s, pl.ds(1, 2)])
            for s in range(S)
        ],
    ]
    fwd_halo = [
        Halo(3 * S + s, fwd_hbm.at[s, 0], fwd.at[s, X + 1, inner, :],
             fwd_hbm.at[s, X - 1], fwd.at[s, 0, inner, :])
        for s in range(S)
    ]
    sig_halo = Halo(4 * S, sigma_hbm.at[pl.ds(0, 2)], sig.at[pl.ds(X + 2, 2), inner, :],
                    sigma_hbm.at[pl.ds(X - 2, 2)], sig.at[pl.ds(0, 2), inner, :])

    def fold(t):
        total = t[:, :LANES]
        for i in range(1, Z // LANES):
            total = total + t[:, LANES * i : LANES * (i + 1)]
        return total

    def sum_copies(slot, count):
        some = pl.ds(0, count)
        return [
            pltpu.make_async_remote_copy(
                psend.at[slot, some], precv.at[slot, k, some],
                sum_send.at[slot, k], sum_recv.at[slot, k],
                device_id={"space": lax.rem(me + k, n)}, device_id_type=MESH)
            for k in range(1, n)
        ]

    def sum_start(slot, *terms):
        for i, t in enumerate(terms):
            psend[slot, i] = fold(t)
        for copy in sum_copies(slot, len(terms)):
            copy.start()

    def sum_finish(slot, count=1):
        totals = [psend[slot, i] for i in range(count)]
        for k, copy in enumerate(sum_copies(slot, count)):
            copy.wait()
            totals = [t + precv[slot, k + 1, i] for i, t in enumerate(totals)]
        totals = [jnp.sum(t, keepdims=True) for t in totals]
        return totals if count > 1 else totals[0]

    def precondition(field, it, s):
        def step(j, carry):
            squares, cross = carry
            sums = [jnp.zeros((ROWS, Z), jnp.float32) for _ in range(X)]
            for p in range(X + 2):
                for b in (-1, 0, 1):
                    v = beside(field, (s, p), j, b)
                    for c in (-1, 0, 1):
                        vc = along(v, c)
                        for a in (-1, 0, 1):
                            x = p - 1 - a
                            if 0 <= x < X:
                                k = 9 * (a + 1) + 3 * (b + 1) + c + 1
                                sums[x] = sums[x] + coef[k, x, plain(j), :] * vc
            for x in range(X):
                if it == 0:
                    smooth[s, x, plain(j), :] = sums[x]
                else:
                    cross = cross + sums[x] * smooth[s, x, plain(j), :]
                squares = squares + sums[x] * sums[x]
            for p in range(X + 2):
                for b in (-1, 0, 1):
                    total = None
                    for c in (-1, 0, 1):
                        given = None
                        for a in (-1, 0, 1):
                            x = p - 1 - a
                            if 0 <= x < X:
                                k = 9 * (a + 1) + 3 * (b + 1) + c + 1
                                term = coef[k, x, plain(j), :] * sums[x]
                                given = term if given is None else given + term
                        given = along(given, -c)
                        total = given if total is None else total + given
                    quart[b + 1, p, padded(j), :] = total
            return squares, cross

        squares, cross = lax.fori_loop(0, tiles, step, (zero, zero))

        def gather(j, carry):
            for p in range(X + 2):
                part[it, s, p, plain(j), :] = (
                    quart[1, p, padded(j), :] + beside(quart, (2, p), j, -1)
                    + beside(quart, (0, p), j, 1))
            return carry

        lax.fori_loop(0, tiles, gather, 0)
        return squares, cross

    def find_weights():
        def step(j, carry):
            for x in range(-1, X + 1):
                here = sig[x + 2, padded(j), :]
                sides = (
                    sig[x + 3, padded(j), :], sig[x + 1, padded(j), :],
                    beside(sig, (x + 2,), j, 1), beside(sig, (x + 2,), j, -1),
                    along(here, 1), along(here, -1))
                diagonal = jnp.full((ROWS, Z), MASS, jnp.float32)
                for i, side in enumerate(sides):
                    w = 0.5 * (here + side)
                    weights[i, x + 1, plain(j), :] = w
                    diagonal = diagonal + w
                weights[6, x + 1, plain(j), :] = diagonal
            return carry

        lax.fori_loop(0, tiles, step, 0)

    def operate(field, s, low, high, keep):
        def step(j, dots):
            for x in range(low, high):
                d = field[s, x + 2, padded(j), :]
                sides = (
                    field[s, x + 3, padded(j), :], field[s, x + 1, padded(j), :],
                    beside(field, (s, x + 2), j, 1), beside(field, (s, x + 2), j, -1),
                    along(d, 1), along(d, -1))
                total = weights[6, x + 1, plain(j), :] * d
                for i, side in enumerate(sides):
                    total = total - weights[i, x + 1, plain(j), :] * side
                if 0 <= x < X:
                    dots = dots + d * total
                if x < 0:
                    total = jnp.where(has_left, total, 0.0)
                if x >= X:
                    total = jnp.where(has_right, total, 0.0)
                if keep:
                    img[s, x + 1, padded(j), :] = total
            return dots

        return lax.fori_loop(0, tiles, step, zero)

    def complete(it, s, x, j):
        total = part[it, s, x + 1, plain(j), :] if -1 <= x <= X else None
        if x < 1:
            there = from_left[it, s, x + 2, plain(j), :]
            if total is not None:
                there = total + there
            total = jnp.where(has_left, there, 0.0 if x < 0 else total)
        if x > X - 2:
            there = from_right[it, s, x - X + 1, plain(j), :]
            if total is not None:
                there = total + there
            total = jnp.where(has_right, there, 0.0 if x >= X else total)
        return total

    def set_first(s):
        def step(j, carry):
            for x in range(-2, X + 2):
                first_dir[s, x + 2, padded(j), :] = complete(0, s, x, j)
            return carry

        lax.fori_loop(0, tiles, step, 0)

    def set_next(s, size, growth):
        def step(j, carry):
            for x in range(-1, X + 1):
                d = first_dir[s, x + 2, padded(j), :]
                next_dir[s, x + 2, padded(j), :] = (
                    (d - size * complete(1, s, x, j)) + growth * d)
            return carry

        lax.fori_loop(0, tiles, step, 0)

    def face_terms(field, s, factor, into, add):
        def step(j, carry):
            for x in range(X):
                f, a = fwd[s, x + 1, padded(j), :], field[s, x + 2, padded(j), :]
                sides = [
                    (r[s, x + at + 1, padded(j), :], r[s, x + at - 1, padded(j), :],
                     beside(r, (s, x + at), j, 1), beside(r, (s, x + at), j, -1),
                     along(v, 1), along(v, -1))
                    for r, v, at in ((fwd, f, 1), (field, a, 2))
                ]
                sums = None
                for fs, as_ in zip(*sides):
                    term = (f - fs) * (a - as_)
                    sums = term if sums is None else sums + term
                term = factor * sums
                if add:
                    term = term + into[x, plain(j), :]
                into[x, plain(j), :] = term
            return carry

        lax.fori_loop(0, tiles, step, 0)

    def add_electrodes(s):
        at = lax.broadcasted_iota(jnp.int32, (ROWS, Z), 0) * Z + lane
        plus = elec[s, 0] - me * (X * H * Z)
        minus = elec[s, 1] - me * (X * H * Z)

        def step(j, carry):
            for x in range(X):
                here = at + (x * H + ROWS * j) * Z
                v = res[s, x + 1, padded(j), :]
                v = v + jnp.where(here == plus, CURRENT, 0.0)
                v = v - jnp.where(here == minus, CURRENT, 0.0)
                res[s, x + 1, padded(j), :] = v
            return carry

        lax.fori_loop(0, tiles, step, 0)

    scale = []
    for s in range(S):
        w = jnp.float32(0.0)
        for i in range(lines.shape[0]):
            w = w + jnp.where(assign[s] == i, lines[i], 0.0)
        scale.append(-0.5 * w)

    for s in range(S):
        load_misfit[s].wait()
        add_electrodes(s)
        res_halo[s].start()
    sig_halo.start()
    fwd_halo[0].start()
    for copy in load_coef:
        copy.wait()

    for s in range(S):
        res_halo[s].arrive()
        squares, _ = precondition(res, 0, s)
        sum_start(s, squares)
        part_halo[0][s].start()
        if s == 0:
            load_sigma.wait()
            sig_halo.arrive()
            find_weights()

    fwd_halo[1].start()
    align, size = [], []
    for s in range(S):
        part_halo[0][s].arrive()
        set_first(s)
        sum_start(S + s, operate(first_dir, s, -1, X + 1, True))
        sum_start(2 * S + s, *precondition(img, 1, s))
        part_halo[1][s].start()

    for s in range(S):
        align.append(sum_finish(s))
        size.append(align[s] / sum_finish(S + s))
    for s in range(S):
        load_fwd[s].wait()
        fwd_halo[s].arrive()
        face_terms(first_dir, s, scale[s] * size[s], gsum, s > 0)

    for s in range(S):
        part_halo[1][s].arrive()
        squares, cross = sum_finish(2 * S + s, 2)
        now = align[s] - size[s] * (2.0 * cross - size[s] * squares)
        set_next(s, size[s], now / align[s])
        align[s] = now
        sum_start(3 * S + s, operate(next_dir, s, 0, X, False))
    for s in range(S):
        face_terms(next_dir, s, scale[s], gpart.at[s], False)

    last_size = [align[s] / sum_finish(3 * S + s) for s in range(S)]

    def combine(j, carry):
        for x in range(X):
            total = gsum[x, plain(j), :]
            for s in range(S):
                total = total + last_size[s] * gpart[s, x, plain(j), :]
            gsum[x, plain(j), :] = total
        return carry

    lax.fori_loop(0, tiles, combine, 0)

    count = H // nsrc

    def share(t):
        return pl.ds(pl.multiple_of(count * t, count), count)

    give = []
    for k in range(1, nsrc):
        to = lax.rem(mine + k, nsrc)
        give.append(pltpu.make_async_remote_copy(
            gsum.at[:, share(to), :], grecv.at[k - 1], grad_send.at[k], grad_recv.at[k],
            device_id={"src": to}, device_id_type=MESH))
        give[-1].start()

    save = []
    for s in range(S):

        def add_up(j, carry, s=s):
            for x in range(X):
                out[s, x, plain(j), :] = (
                    size[s] * first_dir[s, x + 2, padded(j), :]
                    + last_size[s] * next_dir[s, x + 2, padded(j), :])
            return carry

        lax.fori_loop(0, tiles, add_up, 0)
        save.append(pltpu.make_async_copy(out.at[s], adj_hbm.at[s], out_sem.at[s]))
        save[s].start()

    total = gsum[:, share(mine), :]
    for k in range(1, nsrc):
        give[k - 1].wait()
        total = total + grecv[k - 1]
    gout[...] = total
    last = pltpu.make_async_copy(gout, grad_hbm, out_sem.at[S])
    last.start()

    for s in range(S):
        res_halo[s].leave()
        part_halo[0][s].leave()
        part_halo[1][s].leave()
        fwd_halo[s].leave()
        save[s].wait()
    sig_halo.leave()
    last.wait()


def body(n, nsrc, conductivity, inverse_coefficients, forward_potential, misfit_field,
         electrodes, assignment, line_weight):
    S, X, H, Z = misfit_field.shape
    f32 = jnp.float32
    tall = H + 2 * PAD
    field = pltpu.VMEM((S, X + 2, tall, Z), f32)
    wide = pltpu.VMEM((S, X + 4, tall, Z), f32)
    dma = pltpu.SemaphoreType.DMA
    smem = pl.BlockSpec(memory_space=pltpu.SMEM)
    anywhere = pl.BlockSpec(memory_space=pl.ANY)
    shapes = (
        jax.ShapeDtypeStruct((S, X, H, Z), f32),
        jax.ShapeDtypeStruct((X, H // nsrc, Z), f32),
    )
    results = pl.pallas_call(
        functools.partial(kernel, (n, nsrc, S, X, H, Z)),
        out_shape=shapes,
        in_specs=[smem] * 3 + [anywhere] * 4,
        out_specs=(anywhere, anywhere),
        scratch_shapes=[
            pltpu.VMEM((27, X, H, Z), f32),
            pltpu.VMEM((X + 4, tall, Z), f32),
            pltpu.VMEM((7, X + 2, H, Z), f32),
            field, field, field, wide, wide,
            pltpu.VMEM((S, X, H, Z), f32),
            pltpu.VMEM((3, X + 2, tall, Z), f32),
            pltpu.VMEM((ITERS, S, X + 2, H, Z), f32),
            pltpu.VMEM((ITERS, S, 3, H, Z), f32),
            pltpu.VMEM((ITERS, S, 3, H, Z), f32),
            pltpu.VMEM((X, H, Z), f32),
            pltpu.VMEM((S, X, H, Z), f32),
            pltpu.VMEM((S, X, H, Z), f32),
            pltpu.VMEM((nsrc - 1, X, H // nsrc, Z), f32),
            pltpu.VMEM((X, H // nsrc, Z), f32),
            pltpu.VMEM((4 * S, 2, ROWS, LANES), f32),
            pltpu.VMEM((4 * S, n, 2, ROWS, LANES), f32),
            dma((2 * S + 1 + CHUNKS,)),
            dma((S + 1,)),
            dma((4 * S + 1, 2)),
            dma((4 * S + 1, 2)),
            dma((4 * S, n)),
            dma((4 * S, n)),
            dma((nsrc,)),
            dma((nsrc,)),
        ],
        compiler_params=pltpu.CompilerParams(
            collective_id=0, has_side_effects=True, vmem_limit_bytes=60 * 1024 * 1024),
    )(electrodes, assignment, line_weight, conductivity, inverse_coefficients,
      forward_potential, misfit_field)
    return pl.pallas_call(
        hand_over,
        out_shape=shapes,
        in_specs=[pl.BlockSpec(memory_space=pltpu.VMEM)] * 2,
        out_specs=(pl.BlockSpec(memory_space=pltpu.VMEM),) * 2,
    )(*results)


def hand_over(adj, grad, adj_out, grad_out):
    adj_out[...] = adj[...]
    grad_out[...] = grad[...]


def solution(mesh):
    in_specs = (
        P(("groups", "space"), None, None),
        P(None, ("groups", "space"), None, None),
        P(("groups", "src"), "space", None, None),
        P(("groups", "src"), "space", None, None),
        P(("groups", "src"), None),
        P(("groups", "src")),
        P("groups"),
    )
    out_specs = (P(("groups", "src"), "space", None, None), P(("groups", "space"), "src", None))
    run = functools.partial(body, mesh.shape["space"], mesh.shape["src"])
    return jax.shard_map(run, mesh=mesh, in_specs=in_specs, out_specs=out_specs, check_vma=False)
```

time: 49.1 us -> 46.4 us (0.945)
  local copies, waits for them, and re-layouts: 3.34 us -> 0 us
  Pallas kernels: 44.9 us -> 45.6 us
    unnamed x2 -> x0, local copies, waits for them, and re-layouts: 3.34 us -> none
    pallas_call x0 -> x1, Pallas kernels: none -> 1.88 us  [body(): pl.pallas_call(hand_over, out_shape=shapes, in_specs=[pl.BlockSpec(memory...]
    pallas_call x1, Pallas kernels: 44.9 us -> 43.7 us  [body(): pl.pallas_call(functools.partial(kernel, (n, nsrc, S, X, H, Z)), out_shap...]
where the time goes in v2:
time: 46.4 us; the launch traced here: 46.2 us
  Pallas kernels  45.6 us (98%)
  between operations  0.64 us (1%)
    pallas_call x1, Pallas kernels, body(): pl.pallas_call(functools.partial(kernel, (n, nsrc, S, X, H, Z)), out_shap...  43.7 us
    pallas_call x1, Pallas kernels, body(): pl.pallas_call(hand_over, out_shape=shapes, in_specs=[pl.BlockSpec(memory...  1.88 us

profile of v2, /device:TPU:1, one launch (start us, length us, event | category | flops | bytes accessed | tf_op | source)
XLA Modules:
  0.0 46.2 jit_solution(9670299288113116694)
XLA Ops:
  0.6 43.7 %shard_map.86 = (f32[2,4,64,256]{3,2,1,0:T(8,128)}, f32[4,16,256]{2,1,0:T(8,128)}) custom-call(s32[2,2]{1,0:T(2,128)} %elec.1, s32[2]{0:T(128)} %assign.1, f32[4]{0:T(128)} %lines.1, f32[4,64,256]{2,1,0:T(8,128)} %sigma_hbm.1, f32[27,4,64,256]{3,2,1,0:T(8,128)} %coef_hbm.1, f32[2,4,64,256]{3,2,1,0:T(8,128)} %fwd_hbm.1, f32[2,4,64,256]{3,2,1,0:T(8,128)} %misfit_hbm.1), custom_call_target="tpu_custom_call" | custom-call | tf_op jit(solution)/shard_map/pallas_call | solution.py:510
  44.4 1.9 %shard_map.87 = (f32[2,4,64,256]{3,2,1,0:T(8,128)}, f32[4,16,256]{2,1,0:T(8,128)}) custom-call(f32[2,4,64,256]{3,2,1,0:T(8,128)} %get-tuple-element.4.adj, f32[4,16,256]{2,1,0:T(8,128)} %get-tuple-element.5.grad), custom_call_target="tpu_custom_call" | custom-call | tf_op jit(solution)/shard_map/pallas_call | solution.py:545

commit v3 on v2

--- a/solution.py
+++ b/solution.py
@@ -269,7 +269,7 @@
                     + beside(quart, (0, p), j, 1))
             return carry
 
-        lax.fori_loop(0, tiles, gather, 0)
+        lax.fori_loop(0, tiles, gather, 0, unroll=4)
         return squares, cross
 
     def find_weights():
@@ -288,7 +288,7 @@
                 weights[6, x + 1, plain(j), :] = diagonal
             return carry
 
-        lax.fori_loop(0, tiles, step, 0)
+        lax.fori_loop(0, tiles, step, 0, unroll=4)
 
     def operate(field, s, low, high, keep):
         def step(j, dots):
@@ -311,7 +311,7 @@
                     img[s, x + 1, padded(j), :] = total
             return dots
 
-        return lax.fori_loop(0, tiles, step, zero)
+        return lax.fori_loop(0, tiles, step, zero, unroll=4)
 
     def complete(it, s, x, j):
         total = part[it, s, x + 1, plain(j), :] if -1 <= x <= X else None
@@ -333,7 +333,7 @@
                 first_dir[s, x + 2, padded(j), :] = complete(0, s, x, j)
             return carry
 
-        lax.fori_loop(0, tiles, step, 0)
+        lax.fori_loop(0, tiles, step, 0, unroll=4)
 
     def set_next(s, size, growth):
         def step(j, carry):
@@ -343,7 +343,7 @@
                     (d - size * complete(1, s, x, j)) + growth * d)
             return carry
 
-        lax.fori_loop(0, tiles, step, 0)
+        lax.fori_loop(0, tiles, step, 0, unroll=4)
 
     def face_terms(field, s, factor, into, add):
         def step(j, carry):
@@ -365,7 +365,7 @@
                 into[x, plain(j), :] = term
             return carry
 
-        lax.fori_loop(0, tiles, step, 0)
+        lax.fori_loop(0, tiles, step, 0, unroll=4)
 
     def add_electrodes(s):
         at = lax.broadcasted_iota(jnp.int32, (ROWS, Z), 0) * Z + lane
@@ -381,7 +381,7 @@
                 res[s, x + 1, padded(j), :] = v
             return carry
 
-        lax.fori_loop(0, tiles, step, 0)
+        lax.fori_loop(0, tiles, step, 0, unroll=4)
 
     scale = []
     for s in range(S):
@@ -446,7 +446,7 @@
             gsum[x, plain(j), :] = total
         return carry
 
-    lax.fori_loop(0, tiles, combine, 0)
+    lax.fori_loop(0, tiles, combine, 0, unroll=4)
 
     count = H // nsrc
 
@@ -471,7 +471,7 @@
                     + last_size[s] * next_dir[s, x + 2, padded(j), :])
             return carry
 
-        lax.fori_loop(0, tiles, add_up, 0)
+        lax.fori_loop(0, tiles, add_up, 0, unroll=4)
         save.append(pltpu.make_async_copy(out.at[s], adj_hbm.at[s], out_sem.at[s]))
         save[s].start()
 

time: 46.4 us -> 44.7 us (0.963)
  Pallas kernels: 45.6 us -> 43.8 us
    pallas_call x1, Pallas kernels: 43.7 us -> 42 us  [body(): pl.pallas_call(functools.partial(kernel, (n, nsrc, S, X, H, Z)), out_shap...]
where the time goes in v3:
time: 44.7 us; the launch traced here: 44.5 us
  Pallas kernels  43.8 us (98%)
  between operations  0.64 us (1%)
    pallas_call x1, Pallas kernels, body(): pl.pallas_call(functools.partial(kernel, (n, nsrc, S, X, H, Z)), out_shap...  42 us
    pallas_call x1, Pallas kernels, body(): pl.pallas_call(hand_over, out_shape=shapes, in_specs=[pl.BlockSpec(memory...  1.88 us

profile of v3, /device:TPU:1, one launch (start us, length us, event | category | flops | bytes accessed | tf_op | source)
XLA Modules:
  0.0 44.5 jit_solution(13772186442239736761)
XLA Ops:
  0.6 42.0 %shard_map.86 = (f32[2,4,64,256]{3,2,1,0:T(8,128)}, f32[4,16,256]{2,1,0:T(8,128)}) custom-call(s32[2,2]{1,0:T(2,128)} %elec.1, s32[2]{0:T(128)} %assign.1, f32[4]{0:T(128)} %lines.1, f32[4,64,256]{2,1,0:T(8,128)} %sigma_hbm.1, f32[27,4,64,256]{3,2,1,0:T(8,128)} %coef_hbm.1, f32[2,4,64,256]{3,2,1,0:T(8,128)} %fwd_hbm.1, f32[2,4,64,256]{3,2,1,0:T(8,128)} %misfit_hbm.1), custom_call_target="tpu_custom_call" | custom-call | tf_op jit(solution)/shard_map/pallas_call | solution.py:510
  42.6 1.9 %shard_map.87 = (f32[2,4,64,256]{3,2,1,0:T(8,128)}, f32[4,16,256]{2,1,0:T(8,128)}) custom-call(f32[2,4,64,256]{3,2,1,0:T(8,128)} %get-tuple-element.4.adj, f32[4,16,256]{2,1,0:T(8,128)} %get-tuple-element.5.grad), custom_call_target="tpu_custom_call" | custom-call | tf_op jit(solution)/shard_map/pallas_call | solution.py:545
